TPU v7x, 512 devices: a whole 4x8x8 slice. The times are simulated.
512 devices in a mesh: row: 16 (over z_lo, x), col: 8 (over y), fiber: 4 (over z_hi, core).
Axes of the slice: x: 4, y: 8, z: 8 (z_hi: 2, z_lo: 4; z = z_hi * 4 + z_lo), core: 2. Of those that a mesh axis runs over, the one named last changes fastest.
Arguments:
- values: float32 [12288, 12288], P('row', ('col', 'fiber')), may hold values from -6 to 6
- tile_mask: int32 [96, 96], P('row', ('col', 'fiber')), may hold values from 0 to 1, as said below
- keep_mask: int32 [96, 96], P('row', ('col', 'fiber')), may hold values 0 or 1
Outputs:
- flows: float32 [12288, 12288], P('row', ('col', 'fiber'))
Inputs may be any that keep to these rules, and one draw needn't show every extreme that they name: `tile_mask`: 1 marks a tile that holds entries; every diagonal tile is 1, and tiles with low indices are denser.
All inputs are finite; a program needn't handle non-finite values. No bound on the sum of `keep_mask` on one device may be relied on, other than what follows from the above.
Results may differ from a plain program's by a relative error of at most 0.017.
Values may be sent and summed in bfloat16 or wider, within the bound.
No kernel may reach another device: no remote copies, remote signals or barrier semaphores. Data moves between devices by JAX's collectives and lax.ppermute only.
A program may use at most 64 MiB of HBM per device.

v0:
```python
import jax
import jax.numpy as jnp
from jax import lax
from jax.sharding import PartitionSpec as P


def cut_along(shard, dim, peers):
    lengths = shard.shape
    parts = shard.reshape(*lengths[:dim], peers, lengths[dim] // peers, *lengths[dim + 1 :])
    return jnp.moveaxis(parts, dim, 0)


def sum_at_owner(shard, axis, dim):
    parts = cut_along(shard, dim, lax.axis_size(axis))
    arrived = lax.all_to_all(parts, axis, split_axis=0, concat_axis=0, tiled=True)
    return arrived.astype(jnp.float32).sum(axis=0)


def sent_to_all(shard, axis):
    copies = jnp.broadcast_to(shard, (lax.axis_size(axis), *shard.shape))
    return lax.all_to_all(copies, axis, split_axis=0, concat_axis=0, tiled=True)


def taken_together(shard, axis):
    return sent_to_all(shard, axis).sum(axis=0)


def spread_tiles(mask, tile_size):
    count_rows, count_cols = mask.shape
    wide = jnp.broadcast_to(
        mask.astype(jnp.float32)[:, None, :, None], (count_rows, tile_size, count_cols, tile_size)
    )
    return wide.reshape(count_rows * tile_size, count_cols * tile_size)


def local(values, tile_mask, keep_mask):
    n_row = lax.axis_size("row")
    n_fib = lax.axis_size("fiber")
    tile_size = values.shape[1] // tile_mask.shape[1]
    weighted = (values * spread_tiles(tile_mask, tile_size)).astype(jnp.bfloat16)
    rows_dev, unit_width = weighted.shape
    sub_width = unit_width // n_fib
    unit_count = rows_dev // unit_width
    left_stack = weighted.reshape(rows_dev, n_fib, sub_width)
    right_stack = weighted.reshape(unit_count, n_fib, sub_width, unit_width)
    left_recv, right_recv = (
        lax.all_to_all(left_stack, "fiber", split_axis=1, concat_axis=1, tiled=True),
        lax.all_to_all(right_stack, "fiber", split_axis=1, concat_axis=1, tiled=True),
    )
    left_local = left_recv.reshape(rows_dev, unit_width)
    right_local = jnp.transpose(right_recv, (0, 2, 1, 3)).reshape(
        unit_count * sub_width, n_fib * unit_width
    )
    left_all = lax.all_gather(left_local, "col", axis=1, tiled=True)
    partial_product = jnp.dot(
        left_all,
        lax.all_gather(right_local, "row", axis=0, tiled=True),
        preferred_element_type=jnp.float32,
    )
    expanded = sum_at_owner(partial_product.astype(jnp.bfloat16), "fiber", 1)
    squared = expanded * expanded
    col_total = taken_together(jnp.sum(squared, axis=0), "row")
    col_scale = col_total / (rows_dev * n_row) + 1e-06
    return spread_tiles(keep_mask, tile_size) * squared / col_scale[None, :]


def solution(mesh):
    return jax.shard_map(
        local,
        mesh=mesh,
        in_specs=(
            P("row", ("col", "fiber")),
            P("row", ("col", "fiber")),
            P("row", ("col", "fiber")),
        ),
        out_specs=P("row", ("col", "fiber")),
        check_vma=False,
    )
```

profile of v0, /device:TPU:8, one launch (start us, length us, event | category | flops | bytes accessed | tf_op | source)
XLA Modules:
  0.0 311.7 jit_solution(8198016643156649648)
XLA Ops:
  6.5 0.0 all-gather.3.cloned.1.call-start
  6.5 0.7 convert_element_type.16
  7.2 1.6 copy.27
  8.9 0.2 broadcast_in_dim.7
  9.0 0.4 fusion
  9.4 30.0 %all_to_all.21 = bf16[768,4,96]{0,2,1:T(8,128)(2,1)} all-to-all(bf16[768,4,96]{0,2,1:T(8,128)(2,1)S(1)} %bitcast.34), channel_id=1, replica_groups=mesh['row'=16,'col'=8,'fiber'=4] {'fiber'}, dimensions={1} | all-to-all | bytes 1179648 | tf_op jit(solution)/shard_map/all_to_all | solution.py:47
  39.4 0.0 all-gather.3.cloned.1.call-update
  39.4 0.0 all-gather.5.cloned.1.call-start
  39.4 0.3 copy.28
  39.7 0.1 copy.29
  39.8 22.0 %all_to_all.22 = bf16[2,4,96,384]{3,2,0,1:T(8,128)(2,1)S(1)} all-to-all(bf16[2,4,96,384]{3,2,0,1:T(8,128)(2,1)S(1)} %copy.29), channel_id=1, replica_groups=mesh['row'=16,'col'=8,'fiber'=4] {'fiber'}, dimensions={1} | all-to-all | bytes 1179648 | tf_op jit(solution)/shard_map/all_to_all | solution.py:48
  61.9 0.5 copy.30
  62.3 0.9 copy.40
  63.2 0.0 all-gather.5.cloned.1.call-update
  63.2 34.8 %all-gather.3.cloned.1.call-done = bf16[768,3072]{0,1:T(8,128)(2,1)} async-done(((bf16[768,384]{0,1:T(8,128)(2,1)}), bf16[768,3072]{0,1:T(8,128)(2,1)}) %all-gather.3.cloned.1.call-update) | async-done | bytes 4718608 | tf_op jit(solution)/shard_map/all_gather | solution.py:54
  98.0 118.6 %all-gather.5.cloned.1.call-done = bf16[3072,1536]{1,0:T(8,128)(2,1)} async-done(((bf16[192,1536]{1,0:T(8,128)(2,1)}), bf16[3072,1536]{1,0:T(8,128)(2,1)}) %all-gather.5.cloned.1.call-update) | async-done | bytes 9437200 | tf_op jit(solution)/shard_map/all_gather | solution.py:57
  216.6 11.6 %convolution_convert_fusion = bf16[768,1536]{1,0:T(8,128)(2,1)S(1)} fusion(bf16[768,3072]{0,1:T(8,128)(2,1)} %all-gather.3.cloned.1.call-done, bf16[3072,1536]{1,0:T(8,128)(2,1)} %all-gather.5.cloned.1.call-done), kind=kOutput, calls=%fused_computation.1 | convolution fusion | flops 7248936960 | bytes 16515072 | tf_op jit(solution)/shard_map/dot_general | solution.py:55
  228.2 0.2 copy.44
  228.5 61.1 %all_to_all.23 = bf16[4,768,384]{2,1,0:T(8,128)(2,1)S(1)} all-to-all(bf16[4,768,384]{2,1,0:T(8,128)(2,1)S(1)} %bitcast.31), channel_id=1, replica_groups=mesh['row'=16,'col'=8,'fiber'=4] {'fiber'}, dimensions={0} | all-to-all | bytes 4718592 | tf_op jit(solution)/shard_map/all_to_all | solution.py:15
  289.6 0.0 copy-start
  289.6 0.4 convert_reduce_fusion
  289.9 0.1 multiply_reduce_fusion
  290.1 0.6 broadcast_in_dim.8
  290.7 4.1 %all-to-all-start.3 = ((f32[16,1,384]{2,1,0:T(1,128)}), f32[16,1,384]{2,1,0:T(1,128)}, u32[]{:S(2)}, u32[]{:S(2)}) async-start(f32[16,1,384]{2,1,0:T(1,128)} %broadcast_in_dim.8), calls=%async_computation.3 | async-start | bytes 49152 | tf_op jit(solution)/shard_map/all_to_all | solution.py:21
  294.8 0.0 copy-done
  294.9 0.2 broadcast_in_dim.6
  295.0 0.3 copy.45
  295.3 0.4 copy.33
  295.7 7.3 %all-to-all-done.3 = f32[16,1,384]{2,1,0:T(1,128)} async-done(((f32[16,1,384]{2,1,0:T(1,128)}), f32[16,1,384]{2,1,0:T(1,128)}, u32[]{:S(2)}, u32[]{:S(2)}) %all-to-all-start.3) | async-done | bytes 24608 | tf_op jit(solution)/shard_map/all_to_all | solution.py:21
  302.9 0.8 reduce_sum.29
  303.7 1.1 multiply_divide_fusion
  (2 shorter events, 0.0 us)
Async XLA Ops:
  6.5 91.5 %all-gather.3.cloned.1.call-start = ((), (), s32[]{:S(2)}) async-start(), calls=%async_computation.4 | async-start | bytes 5308416 | tf_op jit(solution)/shard_map/all_gather | solution.py:54
  39.4 177.2 %all-gather.5.cloned.1.call-start = ((), (), s32[]{:S(2)}) async-start(), calls=%async_computation.5 | async-start | bytes 10027008 | tf_op jit(solution)/shard_map/all_gather | solution.py:57
  289.6 5.3 %copy-start = (s32[6,3]{0,1:T(4,128)S(1)}, s32[6,3]{0,1:T(4,128)}, u32[]{:S(2)}) copy-start(s32[6,3]{0,1:T(4,128)} %param.5) | copy-start | bytes 220
  290.7 12.2 %all-to-all-start.3 = ((f32[16,1,384]{2,1,0:T(1,128)}), f32[16,1,384]{2,1,0:T(1,128)}, u32[]{:S(2)}, u32[]{:S(2)}) async-start(f32[16,1,384]{2,1,0:T(1,128)} %broadcast_in_dim.8), calls=%async_computation.3 | async-start | bytes 49152 | tf_op jit(solution)/shard_map/all_to_all | solution.py:21
Sparse Core Ops, SparseCore 0:
  39.5 58.4 all-gather.2
  100.1 116.4 all-gather.4
where the time goes:
time: 312 us
  waiting for transfers between devices  161 us (52%)
  blocking collectives  113 us (36%)
  between operations  13.5 us (4%)
  matrix products  11.6 us (4%)
  local copies, waits for them, and re-layouts  5.17 us (2%)
  starting transfers between devices  4.18 us (1%)
  other arithmetic  3.47 us (1%)
    all_gather x1, waiting for transfers between devices, local(): lax.all_gather(right_local, 'row', axis=0, tiled=True)  119 us
    all_to_all x1, blocking collectives, sum_at_owner(): lax.all_to_all(parts, axis, split_axis=0, concat_axis=0, tiled=True)  61.1 us
    all_gather x1, waiting for transfers between devices, local(): left_all = lax.all_gather(left_local, 'col', axis=1, tiled=True)  34.8 us
    all_to_all x1, blocking collectives, local(): lax.all_to_all(left_stack, 'fiber', split_axis=1, concat_axis=1, tiled=True)  30 us
    all_to_all x1, blocking collectives, local(): lax.all_to_all(right_stack, 'fiber', split_axis=1, concat_axis=1, tiled=T...  22 us
    dot_general x1, matrix products, local(): jnp.dot(left_all, lax.all_gather(right_local, 'row', axis=0, tiled=True),...  11.6 us
    all_to_all x1, waiting for transfers between devices, sent_to_all(): return lax.all_to_all(copies, axis, split_axis=0, concat_axis=0, tiled=True)  7.26 us
  transfers between devices with their start and end apart: 3, of which 3 were waited for; matrix products, arithmetic and copies ran while one was open for 1% of the time, Pallas kernels for 0%

commit v1 on v0

--- a/solution.py
+++ b/solution.py
@@ -2,6 +2,12 @@
 import jax.numpy as jnp
 from jax import lax
 from jax.sharding import PartitionSpec as P
+
+
+def gather_by_exchange(x, axis, dim):
+    count = lax.axis_size(axis)
+    repeats = [count if d == dim else 1 for d in range(x.ndim)]
+    return lax.all_to_all(jnp.tile(x, repeats), axis, split_axis=dim, concat_axis=dim, tiled=True)
 
 
 def cut_along(shard, dim, peers):
@@ -51,7 +57,7 @@
     right_local = jnp.transpose(right_recv, (0, 2, 1, 3)).reshape(
         unit_count * sub_width, n_fib * unit_width
     )
-    left_all = lax.all_gather(left_local, "col", axis=1, tiled=True)
+    left_all = gather_by_exchange(left_local, "col", 1)
     partial_product = jnp.dot(
         left_all,
         lax.all_gather(right_local, "row", axis=0, tiled=True),

time: 312 us -> 275 us (0.88)
  the two profiles are of different devices: /device:TPU:8 before, /device:TPU:1 now
where the time goes in v1:
time: 275 us; the launch traced here: 274 us
  blocking collectives  196 us (71%)
  starting transfers between devices  31.6 us (11%)
  between operations  13.5 us (5%)
  local copies, waits for them, and re-layouts  12.5 us (5%)
  matrix products  11.6 us (4%)
  waiting for transfers between devices  6.17 us (2%)
  other arithmetic  3.47 us (1%)
    all_to_all x1, blocking collectives, gather_by_exchange(): lax.all_to_all(jnp.tile(x, repeats), axis, split_axis=dim, concat_axis=di...  111 us
    all_to_all x1, blocking collectives, sum_at_owner(): lax.all_to_all(parts, axis, split_axis=0, concat_axis=0, tiled=True)  38.2 us
    all_to_all x1, starting transfers between devices, sent_to_all(): return lax.all_to_all(copies, axis, split_axis=0, concat_axis=0, tiled=True)  31.6 us
    all_to_all x1, blocking collectives, local(): lax.all_to_all(right_stack, 'fiber', split_axis=1, concat_axis=1, tiled=T...  24.4 us
    all_to_all x1, blocking collectives, local(): lax.all_to_all(left_stack, 'fiber', split_axis=1, concat_axis=1, tiled=True)  22.1 us
    dot_general x1, matrix products, local(): jnp.dot(left_all, lax.all_gather(right_local, 'row', axis=0, tiled=True),...  11.6 us
    all_to_all x1, local copies, waits for them, and re-layouts, gather_by_exchange(): lax.all_to_all(jnp.tile(x, repeats), axis, split_axis=dim, concat_axis=di...  6.63 us
    all_to_all x1, waiting for transfers between devices, sent_to_all(): return lax.all_to_all(copies, axis, split_axis=0, concat_axis=0, tiled=True)  6.15 us
  transfers between devices with their start and end apart: 2, of which 1 were waited for; matrix products, arithmetic and copies ran while one was open for 3% of the time, Pallas kernels for 0%

profile of v1, /device:TPU:1, one launch (start us, length us, event | category | flops | bytes accessed | tf_op | source)
XLA Modules:
  0.0 274.5 jit_solution(17442200153729818719)
XLA Ops:
  6.5 0.0 all-gather.2.cloned.1.call-start
  6.5 0.7 convert_element_type.16
  7.2 1.6 copy.41
  8.9 0.2 broadcast_in_dim.7
  9.0 0.4 fusion
  9.4 0.3 copy.44
  9.7 0.1 copy.45
  9.8 24.4 %all_to_all.30 = bf16[2,4,96,384]{3,2,0,1:T(8,128)(2,1)S(1)} all-to-all(bf16[2,4,96,384]{3,2,0,1:T(8,128)(2,1)S(1)} %copy.45), channel_id=1, replica_groups=mesh['row'=16,'col'=8,'fiber'=4] {'fiber'}, dimensions={1} | all-to-all | bytes 1179648 | tf_op jit(solution)/shard_map/all_to_all | solution.py:54
  34.2 0.5 copy.46
  34.7 0.9 copy.56
  35.6 0.0 all-gather.2.cloned.1.call-update
  35.6 22.1 %all_to_all.31 = bf16[768,4,96]{0,2,1:T(8,128)(2,1)S(1)} all-to-all(bf16[768,4,96]{0,2,1:T(8,128)(2,1)S(1)} %bitcast.35), channel_id=1, replica_groups=mesh['row'=16,'col'=8,'fiber'=4] {'fiber'}, dimensions={1} | all-to-all | bytes 1179648 | tf_op jit(solution)/shard_map/all_to_all | solution.py:53
  57.7 0.3 copy.42
  58.0 0.4 tile.9
  58.5 110.9 %all_to_all.32 = bf16[768,8,384]{2,0,1:T(8,128)(2,1)} all-to-all(bf16[768,8,384]{2,0,1:T(8,128)(2,1)S(1)} %tile.9), channel_id=1, replica_groups=mesh['row'=16,'col'=8,'fiber'=4] {'col'}, dimensions={1} | all-to-all | bytes 9437184 | tf_op jit(solution)/shard_map/all_to_all | solution.py:10
  169.4 6.6 %copy.43 = bf16[768,8,384]{0,2,1:T(8,128)(2,1)} copy(bf16[768,8,384]{2,0,1:T(8,128)(2,1)} %all_to_all.32) | data formatting | bytes 9437184 | tf_op jit(solution)/shard_map/all_to_all | solution.py:10
  176.0 0.0 all-gather.2.cloned.1.call-done
  176.0 11.6 %convolution_convert_fusion = bf16[768,1536]{1,0:T(8,128)(2,1)S(1)} fusion(bf16[768,3072]{0,1:T(8,128)(2,1)} %bitcast.36, bf16[3072,1536]{1,0:T(8,128)(2,1)} %all-gather.2.cloned.1.call-done), kind=kOutput, calls=%fused_computation.1 | convolution fusion | flops 7248936960 | bytes 16515072 | tf_op jit(solution)/shard_map/dot_general | solution.py:61
  187.6 0.2 copy.60
  187.9 38.2 %all_to_all.33 = bf16[4,768,384]{2,1,0:T(8,128)(2,1)S(1)} all-to-all(bf16[4,768,384]{2,1,0:T(8,128)(2,1)S(1)} %bitcast.32), channel_id=1, replica_groups=mesh['row'=16,'col'=8,'fiber'=4] {'fiber'}, dimensions={0} | all-to-all | bytes 4718592 | tf_op jit(solution)/shard_map/all_to_all | solution.py:21
  226.0 0.0 copy-start
  226.0 0.4 convert_reduce_fusion
  226.4 0.1 multiply_reduce_fusion
  226.5 0.6 broadcast_in_dim.8
  227.2 31.6 %all-to-all-start.4 = ((f32[16,1,384]{2,1,0:T(1,128)}), f32[16,1,384]{2,1,0:T(1,128)}, u32[]{:S(2)}, u32[]{:S(2)}) async-start(f32[16,1,384]{2,1,0:T(1,128)} %broadcast_in_dim.8), calls=%async_computation.4 | async-start | bytes 49152 | tf_op jit(solution)/shard_map/all_to_all | solution.py:27
  258.7 0.0 copy-done
  258.8 0.2 broadcast_in_dim.6
  258.9 0.3 copy.61
  259.2 0.4 copy.49
  259.6 6.2 %all-to-all-done.4 = f32[16,1,384]{2,1,0:T(1,128)} async-done(((f32[16,1,384]{2,1,0:T(1,128)}), f32[16,1,384]{2,1,0:T(1,128)}, u32[]{:S(2)}, u32[]{:S(2)}) %all-to-all-start.4) | async-done | bytes 24608 | tf_op jit(solution)/shard_map/all_to_all | solution.py:27
  265.7 0.8 reduce_sum.29
  266.5 1.1 multiply_divide_fusion
  (2 shorter events, 0.0 us)
Async XLA Ops:
  6.5 169.5 %all-gather.2.cloned.1.call-start = ((), (), s32[]{:S(2)}) async-start(), calls=%async_computation.5 | async-start | bytes 10027008 | tf_op jit(solution)/shard_map/all_gather | solution.py:63
  226.0 32.7 %copy-start = (s32[6,3]{0,1:T(4,128)S(1)}, s32[6,3]{0,1:T(4,128)}, u32[]{:S(2)}) copy-start(s32[6,3]{0,1:T(4,128)} %param.5) | copy-start | bytes 220
  227.2 38.6 %all-to-all-start.4 = ((f32[16,1,384]{2,1,0:T(1,128)}), f32[16,1,384]{2,1,0:T(1,128)}, u32[]{:S(2)}, u32[]{:S(2)}) async-start(f32[16,1,384]{2,1,0:T(1,128)} %broadcast_in_dim.8), calls=%async_computation.4 | async-start | bytes 49152 | tf_op jit(solution)/shard_map/all_to_all | solution.py:27
Sparse Core Ops, SparseCore 0:
  35.7 126.3 all-gather.1
